TPU v7x, 32 devices: a whole 2x2x4 slice. The times are simulated.
32 devices in a mesh: grid: 8 (over z, x), cols: 4 (over y, core).
Axes of the slice: x: 2, y: 2, z: 4, core: 2. Of those that a mesh axis runs over, the one named last changes fastest.
Arguments:
- basis: float32 [1024, 3, 16, 1024], P('cols', None, 'grid'), may hold values from -1 to 1
- snapshots: float32 [128, 3, 16, 1024], P('cols', None, 'grid'), may hold values from -60 to 60
- permittivity: float32 [3, 16, 1024], P(None, 'grid'), may hold values from 1 to 10
- labels: int32 [16, 1024], P('grid'), may hold values from 0 to 7
- sigma_table: float32 [8], replicated, may hold values from 0.1 to 10
Outputs:
- new_basis: float32 [128, 3, 16, 1024], P('cols', None, 'grid')
- coefficients: float32 [1024, 128], P('cols')
- cross_terms: float32 [3, 1024, 128], P(None, 'cols')
- block_terms: float32 [3, 128, 128], P(None, 'cols')
All inputs are finite; a program needn't handle non-finite values.
Results may differ from a plain program's by a relative error of at most 0.0003.
Values sent between devices are 32-bit elements; how exact they have to be, the bound alone decides.
A program may use at most 128 MiB of HBM per device.

v0:
```python
import functools

import jax
import jax.numpy as jnp
from jax import lax
from jax.experimental import pallas as pl
from jax.experimental.pallas import tpu as pltpu
from jax.sharding import PartitionSpec as P

NY = 32
LANES = 128
SUBS = 8
CHUNK = 2
BATCHES = 2
PIVOTS = 4
MESH = pl.DeviceIdType.MESH
F32 = jnp.float32
BF16 = jnp.bfloat16


def split(value):
    high = value.astype(BF16)
    return high, (value - high.astype(F32)).astype(BF16)


def dot_nt(left, right):
    return lax.dot_general(
        left, right, (((1,), (1,)), ((), ())), preferred_element_type=F32
    )


def dot_nn(left, right):
    return lax.dot_general(
        left, right, (((1,), (0,)), ((), ())), preferred_element_type=F32
    )


def exact_dot(dot, left, right):
    rows = left.shape[0]
    stacked = jnp.concatenate(split(left), axis=0)
    high, low = right if isinstance(right, tuple) else split(right)
    total = dot(stacked, high) + dot(stacked, low)
    return total[:rows] + total[rows:]


def inverse_factor(rows):
    count = len(rows)
    size = count * SUBS
    shape = (SUBS, size)
    left = list(rows)
    lane = lax.broadcasted_iota(jnp.int32, shape, 1)
    sub = lax.broadcasted_iota(jnp.int32, shape, 0)
    right = [jnp.where(lane == sub + SUBS * i, 1.0, 0.0).astype(F32) for i in range(count)]

    def spread(value):
        return jnp.broadcast_to(value, shape)

    for k in range(0, size, PIVOTS):
        block, first = divmod(k, SUBS)
        row_l = [spread(left[block][first + t : first + t + 1]) for t in range(PIVOTS)]
        row_r = [spread(right[block][first + t : first + t + 1]) for t in range(PIVOTS)]
        pivot = {
            (s, t): spread(row_l[s][:, k + t : k + t + 1])
            for s in range(PIVOTS)
            for t in range(s + 1)
        }
        scale, factor = [], {}
        for t in range(PIVOTS):
            scale.append(lax.rsqrt(pivot[t, t]))
            row_l[t] = row_l[t] * scale[t]
            row_r[t] = row_r[t] * scale[t]
            for s in range(t + 1, PIVOTS):
                factor[s, t] = pivot[s, t] * scale[t]
            for s in range(t + 1, PIVOTS):
                for u in range(t + 1, s + 1):
                    pivot[s, u] = pivot[s, u] - factor[s, t] * factor[u, t]
                row_l[s] = row_l[s] - factor[s, t] * row_l[t]
                row_r[s] = row_r[s] - factor[s, t] * row_r[t]
        for at in range(block, count):
            inside = at == block
            if not inside or first + PIVOTS < SUBS:
                cols = [spread(left[at][:, k + t : k + t + 1]) for t in range(PIVOTS)]
                for t in range(PIVOTS):
                    cols[t] = cols[t] * scale[t]
                    for s in range(t + 1, PIVOTS):
                        cols[s] = cols[s] - factor[s, t] * cols[t]
                if inside:
                    cols = [jnp.where(sub >= first + PIVOTS, c, 0.0) for c in cols]
                for t in range(PIVOTS):
                    left[at] = left[at] - cols[t] * row_l[t]
                    right[at] = right[at] - cols[t] * row_r[t]
            if inside:
                for t in range(PIVOTS):
                    right[at] = jnp.where(sub == first + t, row_r[t], right[at])
    return right


def remote(src, dst, send_sem, recv_sem, peer):
    return pltpu.make_async_remote_copy(
        src_ref=src,
        dst_ref=dst,
        send_sem=send_sem,
        recv_sem=recv_sem,
        device_id=peer,
        device_id_type=MESH,
    )


class Reduction:
    def __init__(self, refs, n, me, peer):
        self.x, self.slots, self.o, self.sems = refs
        self.n, self.me, self.peer = n, me, peer

    def put(self, at, value):
        blocks = self.x.shape[1]
        self.x[at // blocks, at % blocks] = value

    def get(self, at):
        blocks = self.x.shape[1]
        return self.o[at // blocks, at % blocks]

    def scatter(self):
        def body(k, carry):
            q = lax.rem(self.me + k, self.n)
            remote(
                self.x.at[q], self.slots.at[k - 1], self.sems.at[0], self.sems.at[1], self.peer(q)
            ).start()
            return carry

        lax.fori_loop(1, self.n, body, 0)

    def spread(self):
        whole = remote(self.slots, self.slots, self.sems.at[0], self.sems.at[1], self.peer(self.me))
        whole.wait_recv()
        self.o[self.me] = self.x[self.me] + jnp.sum(self.slots[...], axis=0)

        def body(k, carry):
            q = lax.rem(self.me + k, self.n)
            mine = self.o.at[self.me]
            remote(mine, mine, self.sems.at[2], self.sems.at[3], self.peer(q)).start()
            return carry

        lax.fori_loop(1, self.n, body, 0)
        whole.wait_send()

    def finish(self):
        rest = self.o.at[pl.ds(0, self.n - 1)]
        whole = remote(rest, rest, self.sems.at[2], self.sems.at[3], self.peer(self.me))
        whole.wait_recv()
        whole.wait_send()


def reduction_scratch(n, blocks):
    piece = -(-blocks // n)
    shapes = [(n, piece), (n - 1, piece), (n, piece)]
    return [pltpu.VMEM(s + (SUBS, LANES), F32) for s in shapes] + [pltpu.SemaphoreType.DMA((4,))]


def kernel(dims, b_ref, s_ref, eps_ref, lab_ref, sig_ref, *rest):
    (grid_size, cols, own_b, own_s, tiles) = dims
    chips = cols // 2
    n16 = 2 * grid_size
    width = own_s // BATCHES
    q_rows = width * cols
    total_s = own_s * cols
    chip_b = 2 * own_b
    chunks = tiles // CHUNK
    per_col = 6 * tiles
    unknowns = 3 * tiles * LANES * n16

    (nb_ref, coef_ref, cross_ref, block_ref) = rest[:4]
    refs = list(rest[4:])

    def take(count):
        out = refs[:count]
        del refs[:count]
        return out

    (sland, bland, ssend, bsend, brecv, bhi, blo, p, below, above) = take(10)
    (uown, urecv, acc, ct, t_acc, t_send, t_recv, op_hi, op_lo, p2_hi, p2_lo, coef_t) = take(12)
    (m_acc, inv_ref, nb_own, nb_send, nb_recv, sig) = take(6)
    (loc, s_s, s_r, bm_s, bm_r, u_s, u_r, h_s, h_r, t_s, t_r, n_s, n_r) = take(13)

    g = lax.axis_index("grid")
    d = lax.axis_index("cols")
    chip, core = d // 2, lax.rem(d, 2)
    me = 2 * g + core
    mate = (g, 2 * chip + 1 - core)
    far = [lax.rem(chip + k, chips) for k in range(1, chips)]
    same = [(g, 2 * y + core) for y in far]
    cross = [(g, 2 * y + 1 - core) for y in far]

    def line(q):
        return (q // 2, 2 * chip + lax.rem(q, 2))

    def slab(q):
        return (q, d)

    c_sums = [Reduction(take(4), n16, me, line) for _ in range(2 * BATCHES)]
    t_sums = [Reduction(take(4), grid_size, g, slab) for _ in range(BATCHES)]
    g_sum = Reduction(take(4), n16, me, line)
    m_sum = Reduction(take(4), n16, me, line)

    barrier = pltpu.get_barrier_semaphore()

    def greet(k, carry):
        pl.semaphore_signal(
            barrier, inc=1, device_id=line(lax.rem(me + k, n16)), device_id_type=MESH
        )
        return carry

    lax.fori_loop(1, n16, greet, 0)
    for peer in same + cross:
        pl.semaphore_signal(barrier, inc=1, device_id=peer, device_id_type=MESH)

    s_load = pltpu.make_async_copy(s_ref, sland, loc.at[0])
    b_load = pltpu.make_async_copy(b_ref, bland, loc.at[1])
    s_load.start()
    b_load.start()

    zero = jnp.zeros((3, q_rows, LANES), F32)
    for b in range(BATCHES):
        for edge in (0, tiles + 1):
            for buffer in (p, below, above):
                buffer[b, edge] = zero
    for buffer, end in ((below, 0), (above, n16 - 1)):

        @pl.when(me == end)
        def _():
            for b in range(BATCHES):
                buffer[b] = jnp.zeros(buffer.shape[1:], F32)

    layer_rows = pl.ds(0, 2 * tiles)
    region = lab_ref[layer_rows]
    picked = jnp.zeros(region.shape, F32)
    for k in range(sig_ref.shape[0]):
        picked = jnp.where(region == k, sig_ref[k], picked)
    sig[...] = picked

    pl.semaphore_wait(barrier, n16 - 1 + 2 * (chips - 1))

    def mine_of(first, second):
        return jnp.where(core == 0, first, second), jnp.where(core == 0, second, first)

    s_load.wait()
    s_copies = []
    my_cols = pl.ds(pl.multiple_of(d * width, SUBS), width)
    for b in range(BATCHES):

        def sort_s(t, carry):
            for a in range(3):
                layers = []
                for layer in range(2):
                    start = b * width * per_col + (2 * tiles * a + layer) + 2 * t
                    layers.append(sland[pl.ds(start, width, stride=per_col), :])
                own, other = mine_of(*layers)
                p[b, t + 1, a, my_cols, :] = own
                ssend[b, t, a] = other
            return carry

        lax.fori_loop(0, tiles, sort_s, 0)
        landing = p.at[b, pl.ds(1, tiles), :, my_cols, :]
        plan = [(landing, peer) for peer in same]
        plan += [(ssend.at[b], peer) for peer in cross + [mate]]
        for i, (src, peer) in enumerate(plan):
            copy = remote(src, landing, s_s.at[b, i], s_r.at[b, i], peer)
            copy.start()
            s_copies.append((b, copy))

    b_load.wait()

    def b_rows(which):
        return pl.ds(pl.multiple_of(which * own_b, own_b), own_b)

    def put_b(t, a, which, value):
        high, low = split(value)
        lanes = pl.ds(pl.multiple_of((lax.rem(t, CHUNK) * 3 + a) * LANES, LANES), LANES)
        bhi[t // CHUNK, b_rows(which), lanes] = high
        blo[t // CHUNK, b_rows(which), lanes] = low

    def sort_b(t, carry):
        for a in range(3):
            layers = []
            for layer in range(2):
                start = (2 * tiles * a + layer) + 2 * t
                layers.append(bland[pl.ds(start, own_b, stride=per_col), :])
            own, other = mine_of(*layers)
            bsend[t, a] = other
            put_b(t, a, core, own)
        remote(bsend.at[t], brecv.at[t], bm_s.at[t], bm_r.at[t], mate).start()
        return carry

    lax.fori_loop(0, tiles, sort_b, 0)

    def mate_b(t, carry):
        remote(bsend.at[t], brecv.at[t], bm_s.at[t], bm_r.at[t], mate).wait()
        for a in range(3):
            put_b(t, a, 1 - core, brecv[t, a])
        return carry

    lax.fori_loop(0, tiles, mate_b, 0)

    def field_chunk(buffer, j):
        parts = [
            buffer[CHUNK * j + i // 3 + 1, i % 3] for i in range(3 * CHUNK)
        ]
        return jnp.concatenate(parts, axis=1)

    def put_coef(total, sweep, b):
        work = c_sums[sweep * BATCHES + b]
        per_row = chip_b // LANES
        for i in range(q_rows // SUBS):
            for k in range(per_row):
                work.put(
                    i * per_row + k,
                    total[SUBS * i : SUBS * (i + 1), LANES * k : LANES * (k + 1)],
                )
        work.scatter()

    def get_coef(sweep, b):
        work = c_sums[sweep * BATCHES + b]
        work.finish()
        per_row = chip_b // LANES
        rows = []
        for i in range(q_rows // SUBS):
            rows.append(
                jnp.concatenate([work.get(i * per_row + k) for k in range(per_row)], axis=1)
            )
        ct[sweep, b] = jnp.concatenate(rows, axis=0)

    def first_coef(b):
        acc[...] = jnp.zeros_like(acc)

        def body(j, carry):
            acc[...] += exact_dot(dot_nt, field_chunk(p.at[b], j), (bhi[j], blo[j]))
            return carry

        lax.fori_loop(0, chunks, body, 0)
        put_coef(acc[...], 0, b)

    def u_copy(sweep, b, j, k):
        part = pl.ds(CHUNK * j, CHUNK)
        return remote(
            uown.at[sweep, b, part],
            urecv.at[sweep, b, k, part],
            u_s.at[sweep, b, k, j],
            u_r.at[sweep, b, k, j],
            same[k],
        )

    def combine(sweep, b):
        weights = ct[sweep, b]

        def body(j, carry):
            u = exact_dot(dot_nn, weights, (bhi[j], blo[j]))
            for i in range(3 * CHUNK):
                uown[sweep, b, CHUNK * j + i // 3, i % 3] = u[:, LANES * i : LANES * (i + 1)]
            for k in range(chips - 1):
                u_copy(sweep, b, j, k).start()
            return carry

        lax.fori_loop(0, chunks, body, 0)

    def remove(sweep, b, j):
        for k in range(chips - 1):
            u_copy(sweep, b, j, k).wait()
        parts = []
        for i in range(3 * CHUNK):
            t, a = CHUNK * j + i // 3, i % 3
            total = uown[sweep, b, t, a]
            for k in range(chips - 1):
                total = total + urecv[sweep, b, k, t, a]
            left = p[b, t + 1, a] - total
            p[b, t + 1, a] = left
            parts.append(left)
        return parts

    def second_coef(b):
        acc[...] = jnp.zeros_like(acc)

        def body(j, carry):
            field = jnp.concatenate(remove(0, b, j), axis=1)
            acc[...] += exact_dot(dot_nt, field, (bhi[j], blo[j]))
            return carry

        lax.fori_loop(0, chunks, body, 0)
        put_coef(acc[...], 1, b)

    def halo(b, j, up):
        part = pl.ds(CHUNK * j + 1, CHUNK)
        comps = pl.ds(0, 3 if up else 2)
        return remote(
            p.at[b, part, comps],
            (below if up else above).at[b, part, comps],
            h_s.at[b, 0 if up else 1, j],
            h_r.at[b, 0 if up else 1, j],
            line(me + 1 if up else me - 1),
        )

    def final_fields(b):
        def body(j, carry):
            remove(1, b, j)

            @pl.when(me < n16 - 1)
            def _():
                halo(b, j, True).start()

            @pl.when(me > 0)
            def _():
                halo(b, j, False).start()

            return carry

        lax.fori_loop(0, chunks, body, 0)

    def halo_wait(b):
        def body(j, carry):
            @pl.when(me > 0)
            def _():
                halo(b, j, True).wait_recv()
                halo(b, j, False).wait_send()

            @pl.when(me < n16 - 1)
            def _():
                halo(b, j, False).wait_recv()
                halo(b, j, True).wait_send()

            return carry

        lax.fori_loop(0, chunks, body, 0)

    lane = lax.broadcasted_iota(jnp.int32, (q_rows, LANES), 1)
    y_at = lax.rem(lane, NY)

    def yp(f):
        return jnp.where(y_at != NY - 1, pltpu.roll(f, LANES - 1, 1), 0.0)

    def ym(f):
        return jnp.where(y_at != 0, pltpu.roll(f, 1, 1), 0.0)

    def xp(f, after):
        return pltpu.roll(jnp.where(lane < NY, after, f), LANES - NY, 1)

    def xm(f, before):
        return pltpu.roll(jnp.where(lane >= LANES - NY, before, f), NY, 1)

    def curl_tile(b, t):
        at = t + 1
        ex, ey, ez = (p[b, at, a] for a in range(3))
        ex_b, ey_b, ez_b = (p[b, at - 1, a] for a in range(3))
        ey_n, ez_n = p[b, at + 1, 1], p[b, at + 1, 2]
        dx, dy, dz = (below[b, at, a] for a in range(3))
        ux, uy = above[b, at, 0], above[b, at, 1]
        w = ez - dz
        w_n = ez_n - below[b, at + 1, 2]
        ey_x = xp(ey, ey_n)
        v = ey_x - ey
        image_x = 4.0 * ex - yp(ex) - ym(ex + v) + v - ux - dx + xp(w, w_n) - w
        h = ex - xm(ex, ex_b) + w
        image_y = 4.0 * ey - ey_x - xm(ey, ey_b) - uy - dy + yp(h) - h
        du = ux - ex
        du_b = above[b, at - 1, 0] - ex_b
        dv = uy - ey
        image_z = (
            4.0 * ez
            - xp(ez, ez_n)
            - yp(ez)
            - xm(ez + du, ez_b + du_b)
            - ym(ez + dv)
            + du
            + dv
        )
        return [image_x, image_y, image_z]

    def layer_row(ref, row):
        return jnp.where(core == 0, ref[pl.ds(row, 1), :], ref[pl.ds(row + 1, 1), :])

    def operators(b):
        t_acc[...] = jnp.zeros_like(t_acc)

        def body(j, carry):
            images = [[], [], []]
            for c in range(CHUNK):
                t = CHUNK * j + c
                images[0] += curl_tile(b, t)
                loss = layer_row(sig, 2 * t)
                for a in range(3):
                    field = p[b, t + 1, a]
                    images[1].append(field * layer_row(eps_ref, 2 * tiles * a + 2 * t))
                    images[2].append(field * loss)
            stack = jnp.concatenate([jnp.concatenate(i, axis=1) for i in images], axis=0)
            high, low = split(stack)
            op_hi[b, j] = high
            op_lo[b, j] = low
            t_acc[...] += dot_nt(high, bhi[j]) + dot_nt(high, blo[j]) + dot_nt(low, bhi[j])
            return carry

        lax.fori_loop(0, chunks, body, 0)

    def t_copy(b):
        return remote(t_send.at[b], t_recv.at[b], t_s.at[b], t_r.at[b], mate)

    def t_start(b):
        for k in range(3):
            total = t_acc[q_rows * k : q_rows * (k + 1)]
            t_send[b, k] = jnp.where(core == 0, total[:, own_b:], total[:, :own_b])
        t_copy(b).start()

    per_own = own_b // LANES

    def t_scatter(b):
        t_copy(b).wait()
        for k in range(3):
            total = t_acc[q_rows * k : q_rows * (k + 1)]
            mine = jnp.where(core == 0, total[:, :own_b], total[:, own_b:]) + t_recv[b, k]
            for i in range(q_rows // SUBS):
                for c in range(per_own):
                    t_sums[b].put(
                        (k * (q_rows // SUBS) + i) * per_own + c,
                        mine[SUBS * i : SUBS * (i + 1), LANES * c : LANES * (c + 1)],
                    )
        t_sums[b].scatter()

    def in_order(parts):
        rows = []
        for e in range(cols):
            for part in parts:
                rows.append(part[width * e : width * (e + 1)])
        return jnp.concatenate(rows, axis=0)

    def s_wait(b):
        for at, copy in s_copies:
            if at == b:
                copy.wait()

    s_wait(0)
    first_coef(0)
    c_sums[0].spread()
    get_coef(0, 0)
    combine(0, 0)
    s_wait(1)
    first_coef(1)
    c_sums[1].spread()
    get_coef(0, 1)
    combine(0, 1)
    second_coef(0)
    c_sums[2].spread()
    get_coef(1, 0)
    combine(1, 0)
    second_coef(1)
    c_sums[3].spread()
    get_coef(1, 1)
    combine(1, 1)

    coef_t[...] = in_order([ct[0, b] + ct[1, b] for b in range(BATCHES)])
    picked = jnp.where(core == 0, coef_t[:, :own_b], coef_t[:, own_b:])
    coef_ref[...] = picked.T

    final_fields(0)
    halo_wait(0)
    operators(0)
    t_start(0)
    t_scatter(0)
    t_sums[0].spread()

    final_fields(1)

    def gram_body(j, carry):
        field = in_order([field_chunk(p.at[b], j) for b in range(BATCHES)])
        high, low = split(field)
        p2_hi[j] = high
        p2_lo[j] = low
        return carry + dot_nt(high, high) + dot_nt(high, low) + dot_nt(low, high)

    gram = lax.fori_loop(0, chunks, gram_body, jnp.zeros((total_s, total_s), F32))
    for i in range(total_s // SUBS):
        g_sum.put(i, gram[SUBS * i : SUBS * (i + 1)])
    g_sum.scatter()
    halo_wait(1)
    operators(1)
    g_sum.spread()
    t_start(1)

    def m_body(j, carry):
        high, low = p2_hi[j], p2_lo[j]
        for b in range(BATCHES):
            m_acc[b] += (
                dot_nt(op_hi[b, j], high) + dot_nt(op_hi[b, j], low) + dot_nt(op_lo[b, j], high)
            )
        return carry

    m_acc[...] = jnp.zeros_like(m_acc)
    lax.fori_loop(0, chunks, m_body, 0)
    for k in range(3):
        rows = in_order([m_acc[b, q_rows * k : q_rows * (k + 1)] for b in range(BATCHES)])
        for i in range(total_s // SUBS):
            m_sum.put(k * (total_s // SUBS) + i, rows[SUBS * i : SUBS * (i + 1)])
    t_scatter(1)
    m_sum.scatter()
    g_sum.finish()
    gram_rows = [g_sum.get(i) * (1.0 / unknowns) for i in range(total_s // SUBS)]
    for i, value in enumerate(inverse_factor(gram_rows)):
        inv_ref[SUBS * i : SUBS * (i + 1)] = value
    t_sums[1].spread()
    m_sum.spread()

    def own_rows(which):
        return pl.ds(pl.multiple_of(which * own_s, SUBS), own_s)

    inv_own = inv_ref[own_rows(d), :]
    inv_mate = inv_ref[own_rows(2 * chip + 1 - core), :]
    inv_chip = jnp.concatenate([inv_own, inv_mate], axis=0)

    def nb_copy(j):
        part = pl.ds(CHUNK * j, CHUNK)
        return remote(nb_send.at[part], nb_recv.at[part], n_s.at[j], n_r.at[j], mate)

    def nb_body(j, carry):
        value = exact_dot(dot_nn, inv_chip, (p2_hi[j], p2_lo[j]))
        for i in range(3 * CHUNK):
            t, a = CHUNK * j + i // 3, i % 3
            part = value[:, LANES * i : LANES * (i + 1)]
            nb_own[t, a] = part[:own_s]
            nb_send[t, a] = part[own_s:]
        nb_copy(j).start()
        return carry

    lax.fori_loop(0, chunks, nb_body, 0)
    inverse = inv_ref[...]
    inverse_halves = split(inverse)
    for b in range(BATCHES):
        t_sums[b].finish()
    for k in range(3):
        parts = []
        for b in range(BATCHES):
            rows = []
            for i in range(q_rows // SUBS):
                at = (k * (q_rows // SUBS) + i) * per_own
                rows.append(
                    jnp.concatenate([t_sums[b].get(at + c) for c in range(per_own)], axis=1)
                )
            parts.append(jnp.concatenate(rows, axis=0))
        cross_ref[k] = exact_dot(dot_nn, inverse, in_order(parts)).T
    m_sum.finish()
    for k in range(3):
        rows = [m_sum.get(k * (total_s // SUBS) + i) for i in range(total_s // SUBS)]
        half = exact_dot(dot_nn, inv_own, jnp.concatenate(rows, axis=0))
        block_ref[k] = exact_dot(dot_nt, half, inverse_halves) * (1.0 / unknowns)

    def nb_out(j, carry):
        nb_copy(j).wait()
        for i in range(3 * CHUNK):
            t, a = CHUNK * j + i // 3, i % 3
            layers = mine_of(nb_own[t, a], nb_recv[t, a])
            for layer in range(2):
                start = (2 * tiles * a + layer) + 2 * t
                nb_ref[pl.ds(start, own_s, stride=per_col), :] = layers[layer]
        return carry

    lax.fori_loop(0, chunks, nb_out, 0)


def shards(basis, snapshots, permittivity, labels, sigma_table):
    own_b, own_s = basis.shape[0], snapshots.shape[0]
    layers, layer = basis.shape[2:]
    assert layers == 2
    grid_size, cols = lax.axis_size("grid"), lax.axis_size("cols")
    tiles = layer // LANES
    chips = cols // 2
    n16 = 2 * grid_size
    width = own_s // BATCHES
    q_rows = width * cols
    total_s = own_s * cols
    chip_b = 2 * own_b
    chunks = tiles // CHUNK
    depth = CHUNK * 3 * LANES
    per_col = 6 * tiles

    def rows_of(value):
        lead = value.shape[:-2]
        value = value.reshape(lead + (layers, tiles, LANES))
        return jnp.swapaxes(value, -3, -2).reshape(-1, LANES)

    padded = (BATCHES, tiles + 2, 3, q_rows, LANES)
    scratch = [
        pltpu.VMEM((own_s * per_col, LANES), F32),
        pltpu.VMEM((own_b * per_col, LANES), F32),
        pltpu.VMEM((BATCHES, tiles, 3, width, LANES), F32),
        pltpu.VMEM((tiles, 3, own_b, LANES), F32),
        pltpu.VMEM((tiles, 3, own_b, LANES), F32),
        pltpu.VMEM((chunks, chip_b, depth), BF16),
        pltpu.VMEM((chunks, chip_b, depth), BF16),
        pltpu.VMEM(padded, F32),
        pltpu.VMEM(padded, F32),
        pltpu.VMEM(padded, F32),
        pltpu.VMEM((2, BATCHES, tiles, 3, q_rows, LANES), F32),
        pltpu.VMEM((2, BATCHES, chips - 1, tiles, 3, q_rows, LANES), F32),
        pltpu.VMEM((q_rows, chip_b), F32),
        pltpu.VMEM((2, BATCHES, q_rows, chip_b), F32),
        pltpu.VMEM((3 * q_rows, chip_b), F32),
        pltpu.VMEM((BATCHES, 3, q_rows, own_b), F32),
        pltpu.VMEM((BATCHES, 3, q_rows, own_b), F32),
        pltpu.VMEM((BATCHES, chunks, 3 * q_rows, depth), BF16),
        pltpu.VMEM((BATCHES, chunks, 3 * q_rows, depth), BF16),
        pltpu.VMEM((chunks, total_s, depth), BF16),
        pltpu.VMEM((chunks, total_s, depth), BF16),
        pltpu.VMEM((total_s, chip_b), F32),
        pltpu.VMEM((BATCHES, 3 * q_rows, total_s), F32),
        pltpu.VMEM((total_s, total_s), F32),
        pltpu.VMEM((tiles, 3, own_s, LANES), F32),
        pltpu.VMEM((tiles, 3, own_s, LANES), F32),
        pltpu.VMEM((tiles, 3, own_s, LANES), F32),
        pltpu.VMEM((2 * tiles, LANES), F32),
    ]
    sem = pltpu.SemaphoreType.DMA
    scratch += [sem((2,))]
    scratch += [sem((BATCHES, 2 * chips - 1))] * 2
    scratch += [sem((tiles,))] * 2
    scratch += [sem((2, BATCHES, chips - 1, chunks))] * 2
    scratch += [sem((BATCHES, 2, chunks))] * 2
    scratch += [sem((BATCHES,))] * 2
    scratch += [sem((chunks,))] * 2
    vreg = SUBS * LANES
    for _ in range(2 * BATCHES):
        scratch += reduction_scratch(n16, q_rows * chip_b // vreg)
    for _ in range(BATCHES):
        scratch += reduction_scratch(grid_size, 3 * q_rows * own_b // vreg)
    scratch += reduction_scratch(n16, total_s * total_s // vreg)
    scratch += reduction_scratch(n16, 3 * total_s * total_s // vreg)

    vmem = pl.BlockSpec(memory_space=pltpu.VMEM)
    dims = (grid_size, cols, own_b, own_s, tiles)
    new_rows, coefficients, cross_terms, block_terms = pl.pallas_call(
        functools.partial(kernel, dims),
        out_shape=[
            jax.ShapeDtypeStruct((own_s * per_col, LANES), F32),
            jax.ShapeDtypeStruct((own_b, total_s), F32),
            jax.ShapeDtypeStruct((3, own_b, total_s), F32),
            jax.ShapeDtypeStruct((3, own_s, total_s), F32),
        ],
        in_specs=[
            pl.BlockSpec(memory_space=pl.ANY),
            pl.BlockSpec(memory_space=pl.ANY),
            vmem,
            vmem,
            pl.BlockSpec(memory_space=pltpu.SMEM),
        ],
        out_specs=[vmem] * 4,
        scratch_shapes=scratch,
        compiler_params=pltpu.CompilerParams(
            collective_id=0, has_side_effects=True, vmem_limit_bytes=62 << 20
        ),
    )(
        rows_of(basis),
        rows_of(snapshots),
        rows_of(permittivity),
        rows_of(labels),
        sigma_table,
    )
    new_basis = jnp.swapaxes(
        new_rows.reshape(own_s, 3, tiles, layers, LANES), 2, 3
    ).reshape(snapshots.shape)
    return (new_basis, coefficients, cross_terms, block_terms)


def solution(mesh):
    placed = (
        P("cols", None, "grid", None),
        P("cols", None, "grid", None),
        P(None, "grid", None),
        P("grid", None),
        P(),
    )
    return jax.shard_map(
        shards,
        mesh=mesh,
        in_specs=placed,
        out_specs=(
            P("cols", None, "grid", None),
            P("cols", None),
            P(None, "cols", None),
            P(None, "cols", None),
        ),
        check_vma=False,
    )
```

profile of v0, /device:TPU:0, one launch (start us, length us, event | category | flops | bytes accessed | tf_op | source)
XLA Modules:
  0.0 158.8 jit_solution(8405225516406785048)
XLA Ops:
  0.6 151.4 %shard_map.84 = (f32[1536,128]{1,0:T(8,128)}, f32[256,128]{1,0:T(8,128)}, f32[3,256,128]{2,1,0:T(8,128)}, f32[3,32,128]{2,1,0:T(8,128)}) custom-call(f32[12288,128]{1,0:T(8,128)} %bitcast.25, f32[1536,128]{1,0:T(8,128)} %bitcast.26, f32[48,128]{1,0:T(8,128)} %bitcast.28, s32[16,128]{1,0:T(8,128)} %bitcast.29, f32[8]{0:T(128)} %sig_ref.1), custom_call_target="tpu_custom_call" | custom-call | tf_op jit(solution)/shard_map/pallas_call | solution.py:733
  152.0 2.1 %copy.18 = f32[32,3,2,1024]{3,2,1,0:T(2,128)} copy(f32[32,3,2,1024]{3,2,1,0:T(2,128)} %bitcast.27) | data formatting | bytes 1572864
  154.1 1.6 copy.19
  155.7 1.8 %copy.20 = f32[3,256,128]{2,1,0:T(8,128)} copy(f32[3,256,128]{2,1,0:T(8,128)} %get-tuple-element.18) | data formatting | bytes 786432
  157.4 1.4 copy.21
where the time goes:
time: 159 us
  Pallas kernels  151 us (95%)
  local copies, waits for them, and re-layouts  6.82 us (4%)
    pallas_call x1, Pallas kernels, shards(): pl.pallas_call(functools.partial(kernel, dims), out_shape=[jax.ShapeDtype...  151 us
    unnamed x4, local copies, waits for them, and re-layouts  6.82 us

commit v1 on v0

v1 whole, which is shorter than its diff:
```python
import functools

import jax
import jax.numpy as jnp
from jax import lax
from jax.experimental import pallas as pl
from jax.experimental.pallas import tpu as pltpu
from jax.sharding import PartitionSpec as P

NY = 32
LANES = 128
SUBS = 8
CHUNK = 2
PIVOTS = 4
MESH = pl.DeviceIdType.MESH
F32 = jnp.float32
BF16 = jnp.bfloat16


def split(value):
    high = value.astype(BF16)
    return high, (value - high.astype(F32)).astype(BF16)


def dot_nt(left, right):
    return lax.dot_general(
        left, right, (((1,), (1,)), ((), ())), preferred_element_type=F32
    )


def dot_nn(left, right):
    return lax.dot_general(
        left, right, (((1,), (0,)), ((), ())), preferred_element_type=F32
    )


def exact_dot(dot, left, right):
    rows = left.shape[0]
    stacked = jnp.concatenate(split(left), axis=0)
    high, low = right if isinstance(right, tuple) else split(right)
    total = dot(stacked, high) + dot(stacked, low)
    return total[:rows] + total[rows:]


def inverse_factor(rows, between):
    count = len(rows)
    size = count * SUBS
    shape = (SUBS, size)
    left = list(rows)
    lane = lax.broadcasted_iota(jnp.int32, shape, 1)
    sub = lax.broadcasted_iota(jnp.int32, shape, 0)
    right = [jnp.where(lane == sub + SUBS * i, 1.0, 0.0).astype(F32) for i in range(count)]

    def spread(value):
        return jnp.broadcast_to(value, shape)

    for k in range(0, size, PIVOTS):
        if k == size // 4:
            between()
        block, first = divmod(k, SUBS)
        row_l = [spread(left[block][first + t : first + t + 1]) for t in range(PIVOTS)]
        row_r = [spread(right[block][first + t : first + t + 1]) for t in range(PIVOTS)]
        pivot = {
            (s, t): spread(row_l[s][:, k + t : k + t + 1])
            for s in range(PIVOTS)
            for t in range(s + 1)
        }
        scale, factor = [], {}
        for t in range(PIVOTS):
            scale.append(lax.rsqrt(pivot[t, t]))
            row_l[t] = row_l[t] * scale[t]
            row_r[t] = row_r[t] * scale[t]
            for s in range(t + 1, PIVOTS):
                factor[s, t] = pivot[s, t] * scale[t]
            for s in range(t + 1, PIVOTS):
                for u in range(t + 1, s + 1):
                    pivot[s, u] = pivot[s, u] - factor[s, t] * factor[u, t]
                row_l[s] = row_l[s] - factor[s, t] * row_l[t]
                row_r[s] = row_r[s] - factor[s, t] * row_r[t]
        for at in range(block, count):
            inside = at == block
            if not inside or first + PIVOTS < SUBS:
                cols = [spread(left[at][:, k + t : k + t + 1]) for t in range(PIVOTS)]
                for t in range(PIVOTS):
                    cols[t] = cols[t] * scale[t]
                    for s in range(t + 1, PIVOTS):
                        cols[s] = cols[s] - factor[s, t] * cols[t]
                if inside:
                    cols = [jnp.where(sub >= first + PIVOTS, c, 0.0) for c in cols]
                for t in range(PIVOTS):
                    left[at] = left[at] - cols[t] * row_l[t]
                    right[at] = right[at] - cols[t] * row_r[t]
            if inside:
                for t in range(PIVOTS):
                    right[at] = jnp.where(sub == first + t, row_r[t], right[at])
    return right


def remote(src, dst, send_sem, recv_sem, peer):
    return pltpu.make_async_remote_copy(
        src_ref=src,
        dst_ref=dst,
        send_sem=send_sem,
        recv_sem=recv_sem,
        device_id=peer,
        device_id_type=MESH,
    )


class Reduction:
    def __init__(self, refs, n, me, peer):
        self.x, self.slots, self.o, self.sems = refs
        self.n, self.me, self.peer = n, me, peer

    def put(self, at, value):
        blocks = self.x.shape[1]
        self.x[at // blocks, at % blocks] = value

    def get(self, at):
        blocks = self.x.shape[1]
        return self.o[at // blocks, at % blocks]

    def scatter(self):
        def body(k, carry):
            q = lax.rem(self.me + k, self.n)
            remote(
                self.x.at[q], self.slots.at[k - 1], self.sems.at[0], self.sems.at[1], self.peer(q)
            ).start()
            return carry

        lax.fori_loop(1, self.n, body, 0)

    def spread(self):
        whole = remote(self.slots, self.slots, self.sems.at[0], self.sems.at[1], self.peer(self.me))
        whole.wait_recv()
        self.o[self.me] = self.x[self.me] + jnp.sum(self.slots[...], axis=0)

        def body(k, carry):
            q = lax.rem(self.me + k, self.n)
            mine = self.o.at[self.me]
            remote(mine, mine, self.sems.at[2], self.sems.at[3], self.peer(q)).start()
            return carry

        lax.fori_loop(1, self.n, body, 0)
        whole.wait_send()

    def finish(self):
        rest = self.o.at[pl.ds(0, self.n - 1)]
        whole = remote(rest, rest, self.sems.at[2], self.sems.at[3], self.peer(self.me))
        whole.wait_recv()
        whole.wait_send()


def reduction_scratch(n, blocks):
    piece = -(-blocks // n)
    shapes = [(n, piece), (n - 1, piece), (n, piece)]
    return [pltpu.VMEM(s + (SUBS, LANES), F32) for s in shapes] + [pltpu.SemaphoreType.DMA((4,))]


def batch_widths(own_s):
    if own_s % (4 * SUBS) == 0:
        return (own_s // 4, own_s // 2, own_s // 4)
    return (own_s // 2, own_s // 2)


def log2(n):
    bits = n.bit_length() - 1
    assert n == 1 << bits
    return bits


def kernel(dims, b_ref, s_ref, eps_ref, lab_ref, sig_ref, *rest):
    (grid_size, cols, own_b, own_s, tiles) = dims
    chips = cols // 2
    n16 = 2 * grid_size
    bits = log2(n16)
    widths = batch_widths(own_s)
    starts = [sum(widths[:b]) for b in range(len(widths))]
    batches = range(len(widths))
    last = len(widths) - 1
    q_rows = [width * cols for width in widths]
    total_s = own_s * cols
    chip_b = 2 * own_b
    chunks = tiles // CHUNK
    per_col = 6 * tiles
    unknowns = 3 * tiles * LANES * n16

    outs = rest[:4]
    refs = list(rest[4:])

    def take(count):
        out = refs[:count]
        del refs[:count]
        return out

    def each():
        return take(len(widths))

    sland, bland, bsend, brecv, bhi, blo, p2_hi, p2_lo, coef_t, inv_ref = take(10)
    nb_own, nb_send, nb_recv, sig, eps, lab, table, gram_acc = take(8)
    stage = take(4)
    nb_ref, coef_ref, cross_ref, block_ref = stage
    ssend, p, up, below, above = each(), each(), each(), each(), each()
    uown, urecv = [each(), each()], [each(), each()]
    acc, t_acc, t_send, t_recv, op_hi, op_lo, m_acc = (each() for _ in range(7))
    ct = [each(), each()]
    (loc, out_s, s_s, s_r, bm_s, bm_r, u_s, u_r, h_s, h_r, t_s, t_r, n_s, n_r, meet) = take(15)

    g = lax.axis_index("grid")
    d = lax.axis_index("cols")
    chip, core = d // 2, lax.rem(d, 2)
    me = 2 * g + core
    mate = (g, 2 * chip + 1 - core)
    far = [lax.rem(chip + k, chips) for k in range(1, chips)]
    same = [(g, 2 * y + core) for y in far]
    cross = [(g, 2 * y + 1 - core) for y in far]

    def line(q):
        return (q // 2, 2 * chip + lax.rem(q, 2))

    def slab(q):
        return (q, d)

    c_sums = [[Reduction(take(4), n16, me, line) for _ in batches] for _ in range(2)]
    t_sums = [Reduction(take(4), grid_size, g, slab) for _ in batches]
    g_sum = Reduction(take(4), n16, me, line)
    m_sum = Reduction(take(4), n16, me, line)

    partners = [
        line(me + (1 << i) * (1 - 2 * lax.rem(me // (1 << i), 2))) for i in range(bits)
    ]
    barrier = pltpu.get_barrier_semaphore()
    for peer in same + cross + partners:
        pl.semaphore_signal(barrier, inc=1, device_id=peer, device_id_type=MESH)

    def meet_signal(i):
        if i < bits:
            pl.semaphore_signal(meet.at[i], inc=1, device_id=partners[i], device_id_type=MESH)

    def meet_wait(i):
        if i < bits:
            pl.semaphore_wait(meet.at[i], 1)

    loads = [
        pltpu.make_async_copy(src, dst, loc.at[i])
        for i, (src, dst) in enumerate(
            [(s_ref, sland), (b_ref, bland), (eps_ref, eps), (lab_ref, lab), (sig_ref, table)]
        )
    ]
    for load in loads:
        load.start()

    for b in batches:
        zero = jnp.zeros((3, q_rows[b], LANES), F32)
        for edge in (0, tiles + 1):
            p[b][edge] = zero
        above[b][0] = zero[:2]

        @pl.when(me == 0)
        def _():
            below[b][...] = jnp.zeros(below[b].shape, F32)

        @pl.when(me == n16 - 1)
        def _():
            above[b][...] = jnp.zeros(above[b].shape, F32)

    def mine_of(first, second):
        return jnp.where(core == 0, first, second), jnp.where(core == 0, second, first)

    loads[0].wait()

    def my_cols(b):
        return pl.ds(pl.multiple_of(d * widths[b], SUBS), widths[b])

    for b in batches:

        def sort_s(t, carry):
            for a in range(3):
                layers = []
                for layer in range(2):
                    start = starts[b] * per_col + (2 * tiles * a + layer) + 2 * t
                    layers.append(sland[pl.ds(start, widths[b], stride=per_col), :])
                own, other = mine_of(*layers)
                p[b][t + 1, a, my_cols(b), :] = own
                ssend[b][t, a] = other
            return carry

        lax.fori_loop(0, tiles, sort_s, 0)

    pl.semaphore_wait(barrier, 2 * (chips - 1) + bits)
    s_copies = []
    for b in batches:
        landing = p[b].at[pl.ds(1, tiles), :, my_cols(b), :]
        plan = [(landing, peer) for peer in same]
        plan += [(ssend[b], peer) for peer in cross + [mate]]
        for i, (src, peer) in enumerate(plan):
            copy = remote(src, landing, s_s.at[b, i], s_r.at[b, i], peer)
            copy.start()
            s_copies.append((b, copy))
    meet_signal(0)

    def b_rows(which):
        return pl.ds(pl.multiple_of(which * own_b, own_b), own_b)

    def put_b(t, a, which, value):
        high, low = split(value)
        lanes = pl.ds(pl.multiple_of((lax.rem(t, CHUNK) * 3 + a) * LANES, LANES), LANES)
        bhi[t // CHUNK, b_rows(which), lanes] = high
        blo[t // CHUNK, b_rows(which), lanes] = low

    def sort_b(t, carry):
        for a in range(3):
            layers = []
            for layer in range(2):
                start = (2 * tiles * a + layer) + 2 * t
                layers.append(bland[pl.ds(start, own_b, stride=per_col), :])
            own, other = mine_of(*layers)
            bsend[t, a] = other
            put_b(t, a, core, own)
        remote(bsend.at[t], brecv.at[t], bm_s.at[t], bm_r.at[t], mate).start()
        return carry

    loads[1].wait()
    lax.fori_loop(0, tiles, sort_b, 0)
    meet_wait(0)
    meet_signal(1)

    def mate_b(t, carry):
        remote(bsend.at[t], brecv.at[t], bm_s.at[t], bm_r.at[t], mate).wait()
        for a in range(3):
            put_b(t, a, 1 - core, brecv[t, a])
        return carry

    lax.fori_loop(0, tiles // 2, mate_b, 0)
    meet_wait(1)
    meet_signal(2)
    lax.fori_loop(tiles // 2, tiles, mate_b, 0)
    meet_wait(2)
    meet_signal(3)

    for load in loads[2:]:
        load.wait()
    region = lab[...]
    picked = jnp.zeros(region.shape, F32)
    for k in range(sig_ref.shape[0]):
        picked = jnp.where(region == k, table[k], picked)
    sig[...] = picked

    def field_chunk(buffer, j):
        parts = [buffer[CHUNK * j + i // 3 + 1, i % 3] for i in range(3 * CHUNK)]
        return jnp.concatenate(parts, axis=1)

    per_row = chip_b // LANES

    def put_coef(total, sweep, b):
        work = c_sums[sweep][b]
        for i in range(q_rows[b] // SUBS):
            for k in range(per_row):
                work.put(
                    i * per_row + k,
                    total[SUBS * i : SUBS * (i + 1), LANES * k : LANES * (k + 1)],
                )
        work.scatter()

    def get_coef(sweep, b):
        work = c_sums[sweep][b]
        work.finish()
        rows = []
        for i in range(q_rows[b] // SUBS):
            rows.append(
                jnp.concatenate([work.get(i * per_row + k) for k in range(per_row)], axis=1)
            )
        ct[sweep][b][...] = jnp.concatenate(rows, axis=0)

    def descending(body, count=chunks):
        def step(i, carry):
            body(chunks - 1 - i)
            return carry

        lax.fori_loop(0, count, step, 0)

    def first_coef(b):
        acc[b][...] = jnp.zeros_like(acc[b])

        def body(j):
            acc[b][...] += exact_dot(dot_nt, field_chunk(p[b], j), (bhi[j], blo[j]))

        descending(body)
        put_coef(acc[b][...], 0, b)

    def u_copy(sweep, b, j, k):
        part = pl.ds(CHUNK * j, CHUNK)
        return remote(
            uown[sweep][b].at[part],
            urecv[sweep][b].at[k, part],
            u_s.at[sweep, b, k, j],
            u_r.at[sweep, b, k, j],
            same[k],
        )

    def combine(sweep, b):
        weights = ct[sweep][b][...]

        def body(j):
            u = exact_dot(dot_nn, weights, (bhi[j], blo[j]))
            for i in range(3 * CHUNK):
                uown[sweep][b][CHUNK * j + i // 3, i % 3] = u[:, LANES * i : LANES * (i + 1)]
            for k in range(chips - 1):
                u_copy(sweep, b, j, k).start()

        descending(body)

    def remove(sweep, b, j):
        for k in range(chips - 1):
            u_copy(sweep, b, j, k).wait()
        parts = []
        for i in range(3 * CHUNK):
            t, a = CHUNK * j + i // 3, i % 3
            total = uown[sweep][b][t, a]
            for k in range(chips - 1):
                total = total + urecv[sweep][b][k, t, a]
            left = p[b][t + 1, a] - total
            p[b][t + 1, a] = left
            parts.append(left)
        return parts

    def second_coef(b):
        acc[b][...] = jnp.zeros_like(acc[b])

        def body(j):
            field = jnp.concatenate(remove(0, b, j), axis=1)
            acc[b][...] += exact_dot(dot_nt, field, (bhi[j], blo[j]))

        descending(body)
        put_coef(acc[b][...], 1, b)

    lane = lax.broadcasted_iota(jnp.int32, (max(q_rows), LANES), 1)
    y_at = lax.rem(lane, NY)
    y_top, y_low = y_at != NY - 1, y_at != 0
    x_low, x_top = lane < NY, lane >= LANES - NY

    def yp(f):
        return jnp.where(y_top[: f.shape[0]], pltpu.roll(f, LANES - 1, 1), 0.0)

    def ym(f):
        return jnp.where(y_low[: f.shape[0]], pltpu.roll(f, 1, 1), 0.0)

    def xp(f, after):
        return pltpu.roll(jnp.where(x_low[: f.shape[0]], after, f), LANES - NY, 1)

    def xm(f, before):
        return pltpu.roll(jnp.where(x_top[: f.shape[0]], before, f), NY, 1)

    def halo(b, j, to_next):
        part = pl.ds(CHUNK * j, CHUNK)
        shifted = pl.ds(CHUNK * j + 1, CHUNK)
        if to_next:
            src, dst = up[b].at[part], below[b].at[part]
        else:
            src, dst = p[b].at[shifted, pl.ds(0, 2)], above[b].at[shifted]
        at = 0 if to_next else 1
        return remote(
            src, dst, h_s.at[b, at, j], h_r.at[b, at, j], line(me + 1 if to_next else me - 1)
        )

    def finish_field(b, j):
        remove(1, b, j)

        @pl.when(me > 0)
        def _():
            halo(b, j, False).start()

        for c in range(CHUNK):
            t = CHUNK * j + c
            ex, ey, ez = (p[b][t + 1, a] for a in range(3))
            up[b][t, 0] = ex + xp(ez, p[b][t + 2, 2]) - ez
            up[b][t, 1] = ey + yp(ez) - ez

        @pl.when(me < n16 - 1)
        def _():
            halo(b, j, True).start()

    def halo_wait(b, j):
        @pl.when(me > 0)
        def _():
            halo(b, j, True).wait_recv()
            halo(b, j, False).wait_send()

        @pl.when(me < n16 - 1)
        def _():
            halo(b, j, False).wait_recv()
            halo(b, j, True).wait_send()

    def curl_tile(b, t):
        at = t + 1
        ex, ey, ez = (p[b][at, a] for a in range(3))
        ex_b, ey_b, ez_b = (p[b][at - 1, a] for a in range(3))
        ey_x = xp(ey, p[b][at + 1, 1])
        ez_x = xp(ez, p[b][at + 1, 2])
        ux, uy = above[b][at, 0], above[b][at, 1]
        v = ey_x - ey
        image_x = 4.0 * ex - yp(ex) - ym(ex + v) + v - ux - below[b][t, 0] + ez_x - ez
        h = ex - xm(ex, ex_b) + ez
        image_y = 4.0 * ey - ey_x - xm(ey, ey_b) - uy - below[b][t, 1] + yp(h) - h
        du = ux - ex
        du_b = above[b][at - 1, 0] - ex_b
        dv = uy - ey
        image_z = (
            4.0 * ez - ez_x - yp(ez) - xm(ez + du, ez_b + du_b) - ym(ez + dv) + du + dv
        )
        return [image_x, image_y, image_z]

    def layer_row(ref, row):
        return jnp.where(core == 0, ref[pl.ds(row, 1), :], ref[pl.ds(row + 1, 1), :])

    def operators(b, j):
        images = [[], [], []]
        for c in range(CHUNK):
            t = CHUNK * j + c
            images[0] += curl_tile(b, t)
            loss = layer_row(sig, 2 * t)
            for a in range(3):
                field = p[b][t + 1, a]
                images[1].append(field * layer_row(eps, 2 * tiles * a + 2 * t))
                images[2].append(field * loss)
        stack = jnp.concatenate([jnp.concatenate(i, axis=1) for i in images], axis=0)
        high, low = split(stack)
        op_hi[b][j] = high
        op_lo[b][j] = low
        t_acc[b][...] += dot_nt(high, bhi[j]) + dot_nt(high, blo[j]) + dot_nt(low, bhi[j])

    def lagged(b, j):
        halo_wait(b, j - 1)
        operators(b, j)

    def all_operators(b):
        halo_wait(b, chunks - 1)
        descending(functools.partial(lagged, b), chunks - 1)
        operators(b, 0)

    def t_copy(b):
        return remote(t_send[b], t_recv[b], t_s.at[b], t_r.at[b], mate)

    def t_start(b):
        for k in range(3):
            total = t_acc[b][q_rows[b] * k : q_rows[b] * (k + 1)]
            t_send[b][k] = jnp.where(core == 0, total[:, own_b:], total[:, :own_b])
        t_copy(b).start()

    per_own = own_b // LANES

    def t_scatter(b):
        t_copy(b).wait()
        blocks = q_rows[b] // SUBS
        for k in range(3):
            total = t_acc[b][q_rows[b] * k : q_rows[b] * (k + 1)]
            mine = jnp.where(core == 0, total[:, :own_b], total[:, own_b:]) + t_recv[b][k]
            for i in range(blocks):
                for c in range(per_own):
                    t_sums[b].put(
                        (k * blocks + i) * per_own + c,
                        mine[SUBS * i : SUBS * (i + 1), LANES * c : LANES * (c + 1)],
                    )
        t_sums[b].scatter()

    def t_rows(b, k):
        blocks = q_rows[b] // SUBS
        rows = []
        for i in range(blocks):
            at = (k * blocks + i) * per_own
            rows.append(
                jnp.concatenate([t_sums[b].get(at + c) for c in range(per_own)], axis=1)
            )
        return jnp.concatenate(rows, axis=0)

    def in_order(parts):
        rows = []
        for e in range(cols):
            for b in batches:
                rows.append(parts[b][widths[b] * e : widths[b] * (e + 1)])
        return jnp.concatenate(rows, axis=0)

    def gram_chunk(j):
        high, low = split(in_order([field_chunk(p[b], j) for b in batches]))
        p2_hi[j] = high
        p2_lo[j] = low
        gram_acc[...] += dot_nt(high, high) + dot_nt(high, low) + dot_nt(low, high)

    def s_wait(b):
        for at, copy in s_copies:
            if at == b:
                copy.wait()

    writes = {}

    def write(i):
        writes[i] = pltpu.make_async_copy(stage[i], outs[i], out_s.at[i])
        writes[i].start()

    for b in batches:
        s_wait(b)
        if b == 0:
            meet_wait(3)
            for i in range(4, bits):
                meet_signal(i)
                meet_wait(i)
        first_coef(b)
        if b:
            get_coef(0, b - 1)
            combine(0, b - 1)
        c_sums[0][b].spread()
    second_coef(0)
    get_coef(0, last)
    combine(0, last)
    c_sums[1][0].spread()
    get_coef(1, 0)
    combine(1, 0)
    for b in batches[1:]:
        second_coef(b)
        if b > 1:
            get_coef(1, b - 1)
            combine(1, b - 1)
        c_sums[1][b].spread()
    for b in batches:
        t_acc[b][...] = jnp.zeros_like(t_acc[b])
        m_acc[b][...] = jnp.zeros_like(m_acc[b])
    gram_acc[...] = jnp.zeros_like(gram_acc)
    descending(functools.partial(finish_field, 0))
    get_coef(1, last)
    combine(1, last)

    coef_t[...] = in_order([ct[0][b][...] + ct[1][b][...] for b in batches])
    coef_ref[...] = jnp.where(core == 0, coef_t[:, :own_b], coef_t[:, own_b:]).T
    write(1)

    for b in batches[:-1]:
        then = b + 1
        if then != last:
            finish_field(then, chunks - 1)
            all_operators(b)
            t_start(b)
            for j in reversed(range(chunks - 1)):
                finish_field(then, j)
                if j == chunks - 2:
                    t_scatter(b)
                if j == 1:
                    t_sums[b].spread()
        else:

            halo_wait(b, chunks - 1)

            def both(j):
                lagged(b, j)
                finish_field(then, j)
                gram_chunk(j)

            descending(both, chunks - 1)
            operators(b, 0)
            t_start(b)
            finish_field(then, 0)
            gram_chunk(0)
    for i in range(total_s // SUBS):
        g_sum.put(i, gram_acc[SUBS * i : SUBS * (i + 1), :])
    g_sum.scatter()
    t_scatter(last - 1)

    halo_wait(last, chunks - 1)
    descending(functools.partial(lagged, last), chunks - 1)
    g_sum.spread()
    operators(last, 0)
    t_start(last)

    def m_chunk(j):
        high, low = p2_hi[j], p2_lo[j]
        for b in batches:
            m_acc[b][...] += (
                dot_nt(op_hi[b][j], high) + dot_nt(op_hi[b][j], low) + dot_nt(op_lo[b][j], high)
            )

    descending(m_chunk)
    t_scatter(last)
    row_blocks = total_s // SUBS
    for k in range(3):
        rows = in_order([m_acc[b][q_rows[b] * k : q_rows[b] * (k + 1)] for b in batches])
        for i in range(row_blocks):
            m_sum.put(k * row_blocks + i, rows[SUBS * i : SUBS * (i + 1)])
    m_sum.scatter()
    t_sums[last - 1].spread()
    g_sum.finish()

    def between():
        t_sums[last].spread()
        m_sum.spread()

    gram_rows = [g_sum.get(i) * (1.0 / unknowns) for i in range(row_blocks)]
    for i, value in enumerate(inverse_factor(gram_rows, between)):
        inv_ref[SUBS * i : SUBS * (i + 1)] = value

    def own_rows(which):
        return pl.ds(pl.multiple_of(which * own_s, SUBS), own_s)

    inv_own = inv_ref[own_rows(d), :]
    inv_mate = inv_ref[own_rows(2 * chip + 1 - core), :]
    inv_chip = jnp.concatenate([inv_own, inv_mate], axis=0)

    def nb_copy(j):
        part = pl.ds(CHUNK * j, CHUNK)
        return remote(nb_send.at[part], nb_recv.at[part], n_s.at[j], n_r.at[j], mate)

    def nb_body(j):
        value = exact_dot(dot_nn, inv_chip, (p2_hi[j], p2_lo[j]))
        for i in range(3 * CHUNK):
            t, a = CHUNK * j + i // 3, i % 3
            part = value[:, LANES * i : LANES * (i + 1)]
            nb_own[t, a] = part[:own_s]
            nb_send[t, a] = part[own_s:]
        nb_copy(j).start()

    descending(nb_body)
    inverse = inv_ref[...]
    inverse_halves = split(inverse)
    for b in batches:
        t_sums[b].finish()
    for k in range(3):
        cross_ref[k] = exact_dot(dot_nn, inverse, in_order([t_rows(b, k) for b in batches])).T
    write(2)

    def nb_out(j):
        nb_copy(j).wait()
        for i in range(3 * CHUNK):
            t, a = CHUNK * j + i // 3, i % 3
            layers = mine_of(nb_own[t, a], nb_recv[t, a])
            for layer in range(2):
                start = (2 * tiles * a + layer) + 2 * t
                nb_ref[pl.ds(start, own_s, stride=per_col), :] = layers[layer]

    descending(nb_out)
    write(0)
    m_sum.finish()
    for k in range(3):
        rows = [m_sum.get(k * row_blocks + i) for i in range(row_blocks)]
        half = exact_dot(dot_nn, inv_own, jnp.concatenate(rows, axis=0))
        block_ref[k] = exact_dot(dot_nt, half, inverse_halves) * (1.0 / unknowns)
    write(3)
    for copy in writes.values():
        copy.wait()


def hand_over(*refs):
    sources, targets, held, sems = refs[:4], refs[4:8], refs[8:12], refs[12]
    reads = [pltpu.make_async_copy(sources[i], held[i], sems.at[0, i]) for i in range(4)]
    writes = [pltpu.make_async_copy(held[i], targets[i], sems.at[1, i]) for i in range(4)]
    for copy in reads:
        copy.start()
    for read, copy in zip(reads, writes):
        read.wait()
        copy.start()
    for copy in writes:
        copy.wait()


def shards(basis, snapshots, permittivity, labels, sigma_table):
    own_b, own_s = basis.shape[0], snapshots.shape[0]
    layers, layer = basis.shape[2:]
    assert layers == 2
    grid_size, cols = lax.axis_size("grid"), lax.axis_size("cols")
    tiles = layer // LANES
    chips = cols // 2
    n16 = 2 * grid_size
    widths = batch_widths(own_s)
    q_rows = [width * cols for width in widths]
    total_s = own_s * cols
    chip_b = 2 * own_b
    chunks = tiles // CHUNK
    depth = CHUNK * 3 * LANES
    per_col = 6 * tiles
    count = len(widths)

    def rows_of(value):
        lead = value.shape[:-2]
        value = value.reshape(lead + (layers, tiles, LANES))
        return jnp.swapaxes(value, -3, -2).reshape(-1, LANES)

    def vmem(*shape, dtype=F32):
        return pltpu.VMEM(shape, dtype)

    out_shapes = [
        (own_s * per_col, LANES),
        (own_b, total_s),
        (3, own_b, total_s),
        (3, own_s, total_s),
    ]
    scratch = [
        vmem(own_s * per_col, LANES),
        vmem(own_b * per_col, LANES),
        vmem(tiles, 3, own_b, LANES),
        vmem(tiles, 3, own_b, LANES),
        vmem(chunks, chip_b, depth, dtype=BF16),
        vmem(chunks, chip_b, depth, dtype=BF16),
        vmem(chunks, total_s, depth, dtype=BF16),
        vmem(chunks, total_s, depth, dtype=BF16),
        vmem(total_s, chip_b),
        vmem(total_s, total_s),
    ]
    scratch += [vmem(tiles, 3, own_s, LANES)] * 3
    scratch += [vmem(layers * tiles, LANES), vmem(3 * layers * tiles, LANES)]
    scratch += [vmem(layers * tiles, LANES, dtype=labels.dtype)]
    scratch += [pltpu.SMEM(sigma_table.shape, F32), vmem(total_s, total_s)]
    scratch += [vmem(*shape) for shape in out_shapes]
    scratch += [vmem(tiles, 3, width, LANES) for width in widths]
    scratch += [vmem(tiles + 2, 3, q, LANES) for q in q_rows]
    scratch += [vmem(tiles, 2, q, LANES) for q in q_rows] * 2
    scratch += [vmem(tiles + 1, 2, q, LANES) for q in q_rows]
    scratch += [vmem(tiles, 3, q, LANES) for q in q_rows] * 2
    scratch += [vmem(chips - 1, tiles, 3, q, LANES) for q in q_rows] * 2
    scratch += [vmem(q, chip_b) for q in q_rows]
    scratch += [vmem(3 * q, chip_b) for q in q_rows]
    scratch += [vmem(3, q, own_b) for q in q_rows] * 2
    scratch += [vmem(chunks, 3 * q, depth, dtype=BF16) for q in q_rows] * 2
    scratch += [vmem(3 * q, total_s) for q in q_rows]
    scratch += [vmem(q, chip_b) for q in q_rows] * 2
    sem = pltpu.SemaphoreType.DMA
    scratch += [sem((5,)), sem((4,))]
    scratch += [sem((count, 2 * chips - 1))] * 2
    scratch += [sem((tiles,))] * 2
    scratch += [sem((2, count, chips - 1, chunks))] * 2
    scratch += [sem((count, 2, chunks))] * 2
    scratch += [sem((count,))] * 2
    scratch += [sem((chunks,))] * 2
    scratch += [pltpu.SemaphoreType.REGULAR((log2(n16),))]
    vreg = SUBS * LANES
    for _ in range(2):
        for q in q_rows:
            scratch += reduction_scratch(n16, q * chip_b // vreg)
    for q in q_rows:
        scratch += reduction_scratch(grid_size, 3 * q * own_b // vreg)
    scratch += reduction_scratch(n16, total_s * total_s // vreg)
    scratch += reduction_scratch(n16, 3 * total_s * total_s // vreg)

    anywhere = pl.BlockSpec(memory_space=pl.ANY)
    outputs = [jax.ShapeDtypeStruct(shape, F32) for shape in out_shapes]
    dims = (grid_size, cols, own_b, own_s, tiles)
    results = pl.pallas_call(
        functools.partial(kernel, dims),
        out_shape=outputs,
        in_specs=[anywhere] * 5,
        out_specs=[anywhere] * 4,
        scratch_shapes=scratch,
        compiler_params=pltpu.CompilerParams(
            collective_id=0, has_side_effects=True, vmem_limit_bytes=62 << 20
        ),
    )(
        rows_of(basis),
        rows_of(snapshots),
        rows_of(permittivity),
        rows_of(labels),
        sigma_table,
    )
    new_rows, coefficients, cross_terms, block_terms = pl.pallas_call(
        hand_over,
        out_shape=outputs,
        in_specs=[anywhere] * 4,
        out_specs=[anywhere] * 4,
        scratch_shapes=[vmem(*shape) for shape in out_shapes] + [sem((2, 4))],
    )(*results)
    new_basis = jnp.swapaxes(
        new_rows.reshape(own_s, 3, tiles, layers, LANES), 2, 3
    ).reshape(snapshots.shape)
    return (new_basis, coefficients, cross_terms, block_terms)


def solution(mesh):
    placed = (
        P("cols", None, "grid", None),
        P("cols", None, "grid", None),
        P(None, "grid", None),
        P("grid", None),
        P(),
    )
    return jax.shard_map(
        shards,
        mesh=mesh,
        in_specs=placed,
        out_specs=(
            P("cols", None, "grid", None),
            P("cols", None),
            P(None, "cols", None),
            P(None, "cols", None),
        ),
        check_vma=False,
    )
```

time: 159 us -> 129 us (0.81)
  Pallas kernels: 151 us -> 128 us
  local copies, waits for them, and re-layouts: 6.82 us -> 0 us
    pallas_call x1 -> x2, Pallas kernels: 151 us -> 128 us  [the longest x1 126 us: shards(): pl.pallas_call(functools.partial(kernel, dims), out_shape=outputs, in_spe...]
    unnamed x4 -> x0, local copies, waits for them, and re-layouts: 6.82 us -> none
where the time goes in v1:
time: 129 us
  Pallas kernels  128 us (99%)
    pallas_call x1, Pallas kernels, shards(): pl.pallas_call(functools.partial(kernel, dims), out_shape=outputs, in_spe...  126 us

profile of v1, /device:TPU:0, one launch (start us, length us, event | category | flops | bytes accessed | tf_op | source)
XLA Modules:
  0.0 128.6 jit_solution(2967206929099741476)
XLA Ops:
  0.6 125.6 %shard_map.84 = (f32[1536,128]{1,0:T(8,128)}, f32[256,128]{1,0:T(8,128)}, f32[3,256,128]{2,1,0:T(8,128)}, f32[3,32,128]{2,1,0:T(8,128)}) custom-call(f32[12288,128]{1,0:T(8,128)} %bitcast.25, f32[1536,128]{1,0:T(8,128)} %bitcast.26, f32[48,128]{1,0:T(8,128)} %bitcast.27, s32[16,128]{1,0:T(8,128)} %bitcast.28, f32[8]{0:T(128)} %sig_ref.1), custom_call_target="tpu_custom_call" | custom-call | tf_op jit(solution)/shard_map/pallas_call | solution.py:843
  126.2 2.3 %shard_map.85 = (f32[1536,128]{1,0:T(8,128)}, f32[256,128]{1,0:T(8,128)}, f32[3,256,128]{2,1,0:T(8,128)}, f32[3,32,128]{2,1,0:T(8,128)}) custom-call(f32[1536,128]{1,0:T(8,128)} %get-tuple-element.12.refs_0_, f32[256,128]{1,0:T(8,128)} %get-tuple-element.13.refs_1_, f32[3,256,128]{2,1,0:T(8,128)} %get-tuple-element.14.refs_2_, ...), custom_call_target="tpu_custom_call" | custom-call | tf_op jit(solution)/shard_map/pallas_call | solution.py:859

commit v2 on v1

--- a/solution.py
+++ b/solution.py
@@ -55,7 +55,7 @@
         return jnp.broadcast_to(value, shape)
 
     for k in range(0, size, PIVOTS):
-        if k == size // 4:
+        if k == size // 2:
             between()
         block, first = divmod(k, SUBS)
         row_l = [spread(left[block][first + t : first + t + 1]) for t in range(PIVOTS)]
@@ -224,7 +224,8 @@
     c_sums = [[Reduction(take(4), n16, me, line) for _ in batches] for _ in range(2)]
     t_sums = [Reduction(take(4), grid_size, g, slab) for _ in batches]
     g_sum = Reduction(take(4), n16, me, line)
-    m_sum = Reduction(take(4), n16, me, line)
+    m_sum = Reduction(take(4), grid_size, g, slab)
+    m_send, m_recv, m_got, m_sems = take(4)
 
     partners = [
         line(me + (1 << i) * (1 - 2 * lax.rem(me // (1 << i), 2))) for i in range(bits)
@@ -585,6 +586,13 @@
         p2_hi[j] = high
         p2_lo[j] = low
         gram_acc[...] += dot_nt(high, high) + dot_nt(high, low) + dot_nt(low, high)
+
+    def m_chunk(rows_of, j):
+        high, low = p2_hi[j], p2_lo[j]
+        for b in rows_of:
+            m_acc[b][...] += (
+                dot_nt(op_hi[b][j], high) + dot_nt(op_hi[b][j], low) + dot_nt(op_lo[b][j], high)
+            )
 
     def s_wait(b):
         for at, copy in s_copies:
@@ -653,6 +661,7 @@
                 lagged(b, j)
                 finish_field(then, j)
                 gram_chunk(j)
+                m_chunk(batches[:-1], j)
 
             descending(both, chunks - 1)
             operators(b, 0)
@@ -663,6 +672,7 @@
         g_sum.put(i, gram_acc[SUBS * i : SUBS * (i + 1), :])
     g_sum.scatter()
     t_scatter(last - 1)
+    m_chunk(batches[:-1], 0)
 
     halo_wait(last, chunks - 1)
     descending(functools.partial(lagged, last), chunks - 1)
@@ -670,20 +680,23 @@
     operators(last, 0)
     t_start(last)
 
-    def m_chunk(j):
-        high, low = p2_hi[j], p2_lo[j]
-        for b in batches:
-            m_acc[b][...] += (
-                dot_nt(op_hi[b][j], high) + dot_nt(op_hi[b][j], low) + dot_nt(op_lo[b][j], high)
-            )
-
-    descending(m_chunk)
-    t_scatter(last)
-    row_blocks = total_s // SUBS
+    descending(functools.partial(m_chunk, [last]))
+    half_s = total_s // 2
+    m_halves = []
     for k in range(3):
         rows = in_order([m_acc[b][q_rows[b] * k : q_rows[b] * (k + 1)] for b in batches])
-        for i in range(row_blocks):
-            m_sum.put(k * row_blocks + i, rows[SUBS * i : SUBS * (i + 1)])
+        mine, other = mine_of(rows[:half_s], rows[half_s:])
+        m_send[k] = other
+        m_halves.append(mine)
+    m_copy = remote(m_send, m_recv, m_sems.at[0], m_sems.at[1], mate)
+    m_copy.start()
+    t_scatter(last)
+    m_copy.wait()
+    half_blocks = half_s // SUBS
+    for k in range(3):
+        total = m_halves[k] + m_recv[k]
+        for i in range(half_blocks):
+            m_sum.put(k * half_blocks + i, total[SUBS * i : SUBS * (i + 1)])
     m_sum.scatter()
     t_sums[last - 1].spread()
     g_sum.finish()
@@ -692,6 +705,7 @@
         t_sums[last].spread()
         m_sum.spread()
 
+    row_blocks = total_s // SUBS
     gram_rows = [g_sum.get(i) * (1.0 / unknowns) for i in range(row_blocks)]
     for i, value in enumerate(inverse_factor(gram_rows, between)):
         inv_ref[SUBS * i : SUBS * (i + 1)] = value
@@ -719,11 +733,6 @@
     descending(nb_body)
     inverse = inv_ref[...]
     inverse_halves = split(inverse)
-    for b in batches:
-        t_sums[b].finish()
-    for k in range(3):
-        cross_ref[k] = exact_dot(dot_nn, inverse, in_order([t_rows(b, k) for b in batches])).T
-    write(2)
 
     def nb_out(j):
         nb_copy(j).wait()
@@ -738,8 +747,20 @@
     write(0)
     m_sum.finish()
     for k in range(3):
-        rows = [m_sum.get(k * row_blocks + i) for i in range(row_blocks)]
-        half = exact_dot(dot_nn, inv_own, jnp.concatenate(rows, axis=0))
+        rows = [m_sum.get(k * half_blocks + i) for i in range(half_blocks)]
+        m_send[k] = jnp.concatenate(rows, axis=0)
+    m_back = remote(m_send, m_got, m_sems.at[2], m_sems.at[3], mate)
+    m_back.start()
+    for b in batches:
+        t_sums[b].finish()
+    for k in range(3):
+        cross_ref[k] = exact_dot(dot_nn, inverse, in_order([t_rows(b, k) for b in batches])).T
+    write(2)
+
+    m_back.wait()
+    for k in range(3):
+        rows = jnp.concatenate(mine_of(m_send[k], m_got[k]), axis=0)
+        half = exact_dot(dot_nn, inv_own, rows)
         block_ref[k] = exact_dot(dot_nt, half, inverse_halves) * (1.0 / unknowns)
     write(3)
     for copy in writes.values():
@@ -835,7 +856,8 @@
     for q in q_rows:
         scratch += reduction_scratch(grid_size, 3 * q * own_b // vreg)
     scratch += reduction_scratch(n16, total_s * total_s // vreg)
-    scratch += reduction_scratch(n16, 3 * total_s * total_s // vreg)
+    scratch += reduction_scratch(grid_size, 3 * total_s * total_s // 2 // vreg)
+    scratch += [vmem(3, total_s // 2, total_s)] * 3 + [sem((4,))]
 
     anywhere = pl.BlockSpec(memory_space=pl.ANY)
     outputs = [jax.ShapeDtypeStruct(shape, F32) for shape in out_shapes]

time: 129 us -> 125 us (0.969)
  Pallas kernels: 128 us -> 124 us
    pallas_call x1, Pallas kernels: 126 us -> 122 us  [shards(): pl.pallas_call(functools.partial(kernel, dims), out_shape=outputs, in_spe...]
where the time goes in v2:
time: 125 us
  Pallas kernels  124 us (99%)
    pallas_call x1, Pallas kernels, shards(): pl.pallas_call(functools.partial(kernel, dims), out_shape=outputs, in_spe...  122 us

profile of v2, /device:TPU:0, one launch (start us, length us, event | category | flops | bytes accessed | tf_op | source)
XLA Modules:
  0.0 125.2 jit_solution(5874719951344865941)
XLA Ops:
  0.6 122.2 %shard_map.84 = (f32[1536,128]{1,0:T(8,128)}, f32[256,128]{1,0:T(8,128)}, f32[3,256,128]{2,1,0:T(8,128)}, f32[3,32,128]{2,1,0:T(8,128)}) custom-call(f32[12288,128]{1,0:T(8,128)} %bitcast.25, f32[1536,128]{1,0:T(8,128)} %bitcast.26, f32[48,128]{1,0:T(8,128)} %bitcast.27, s32[16,128]{1,0:T(8,128)} %bitcast.28, f32[8]{0:T(128)} %sig_ref.1), custom_call_target="tpu_custom_call" | custom-call | tf_op jit(solution)/shard_map/pallas_call | solution.py:865
  122.8 2.3 %shard_map.85 = (f32[1536,128]{1,0:T(8,128)}, f32[256,128]{1,0:T(8,128)}, f32[3,256,128]{2,1,0:T(8,128)}, f32[3,32,128]{2,1,0:T(8,128)}) custom-call(f32[1536,128]{1,0:T(8,128)} %get-tuple-element.12.refs_0_, f32[256,128]{1,0:T(8,128)} %get-tuple-element.13.refs_1_, f32[3,256,128]{2,1,0:T(8,128)} %get-tuple-element.14.refs_2_, ...), custom_call_target="tpu_custom_call" | custom-call | tf_op jit(solution)/shard_map/pallas_call | solution.py:881

commit v3 on v2

--- a/solution.py
+++ b/solution.py
@@ -55,7 +55,7 @@
         return jnp.broadcast_to(value, shape)
 
     for k in range(0, size, PIVOTS):
-        if k == size // 2:
+        if k == size * 3 // 4:
             between()
         block, first = divmod(k, SUBS)
         row_l = [spread(left[block][first + t : first + t + 1]) for t in range(PIVOTS)]
@@ -142,9 +142,10 @@
             return carry
 
         lax.fori_loop(1, self.n, body, 0)
-        whole.wait_send()
 
     def finish(self):
+        sent = remote(self.slots, self.slots, self.sems.at[0], self.sems.at[1], self.peer(self.me))
+        sent.wait_send()
         rest = self.o.at[pl.ds(0, self.n - 1)]
         whole = remote(rest, rest, self.sems.at[2], self.sems.at[3], self.peer(self.me))
         whole.wait_recv()

time: 125 us -> 125 us (level)
  no operation moved by 1% of the time
where the time goes in v3:
time: 125 us
  Pallas kernels  124 us (99%)
    pallas_call x1, Pallas kernels, shards(): pl.pallas_call(functools.partial(kernel, dims), out_shape=outputs, in_spe...  122 us

profile of v3, /device:TPU:0, one launch (start us, length us, event | category | flops | bytes accessed | tf_op | source)
XLA Modules:
  0.0 125.3 jit_solution(16603354512836177938)
XLA Ops:
  0.6 122.2 %shard_map.84 = (f32[1536,128]{1,0:T(8,128)}, f32[256,128]{1,0:T(8,128)}, f32[3,256,128]{2,1,0:T(8,128)}, f32[3,32,128]{2,1,0:T(8,128)}) custom-call(f32[12288,128]{1,0:T(8,128)} %bitcast.25, f32[1536,128]{1,0:T(8,128)} %bitcast.26, f32[48,128]{1,0:T(8,128)} %bitcast.27, s32[16,128]{1,0:T(8,128)} %bitcast.28, f32[8]{0:T(128)} %sig_ref.1), custom_call_target="tpu_custom_call" | custom-call | tf_op jit(solution)/shard_map/pallas_call | solution.py:866
  122.8 2.3 %shard_map.85 = (f32[1536,128]{1,0:T(8,128)}, f32[256,128]{1,0:T(8,128)}, f32[3,256,128]{2,1,0:T(8,128)}, f32[3,32,128]{2,1,0:T(8,128)}) custom-call(f32[1536,128]{1,0:T(8,128)} %get-tuple-element.12.refs_0_, f32[256,128]{1,0:T(8,128)} %get-tuple-element.13.refs_1_, f32[3,256,128]{2,1,0:T(8,128)} %get-tuple-element.14.refs_2_, ...), custom_call_target="tpu_custom_call" | custom-call | tf_op jit(solution)/shard_map/pallas_call | solution.py:882
